TPU v7x, 128 devices: a whole 4x4x4 slice. The times are simulated.
128 devices in a mesh: replica: 8 (over x, z_lo), section: 8 (over y, z_hi), tensor: 2 (over core).
Axes of the slice: x: 4, y: 4, z: 4 (z_hi: 2, z_lo: 2; z = z_hi * 2 + z_lo), core: 2. Of those that a mesh axis runs over, the one named last changes fastest.
Arguments:
- base_weights: bfloat16 [8, 8192, 512], P('section', None, 'tensor'), may hold values from -6 to 6
- local_weights: bfloat16 [8, 8, 8192, 512], P('replica', 'section', None, 'tensor'), may hold values from -6 to 6
- outer_momentum: float32 [8, 8192, 512], P('section', 'replica', 'tensor'), may hold values from -6 to 6
- scale_exponents: int32 [8, 256, 512], P('section', None, 'tensor'), may hold values from -1 to 1
- section_inputs: bfloat16 [8, 8, 1280, 8192], P('replica', 'section', 'tensor'), may hold values from -6 to 6
- norm_gain: float32 [8, 8192], P('section'), may hold values from 0.1 to 1.9
Outputs:
- new_base: bfloat16 [8, 8192, 512], P('section', None, 'tensor')
- new_momentum: float32 [8, 8192, 512], P('section', 'replica', 'tensor')
- key_out: bfloat16 [8, 8, 1280, 512], P('replica', 'section', 'tensor')
All inputs are finite; a program needn't handle non-finite values.
Results may differ from a plain program's by a relative error of at most 0.0049.
Values may be sent and summed in bfloat16 or wider, within the bound.
A program may use at most 192 MiB of HBM per device.

v0:
```python
import jax
import jax.numpy as jnp
from jax import lax
from jax.sharding import PartitionSpec as P

D = 8192


OUTER_RATE = 0.7
MOMENTUM_DECAY = 0.9
NORM_EPSILON = 1e-05


def passed_along(shard, axis, by):
    size = lax.axis_size(axis)
    return lax.ppermute(shard, axis, [(i, (i + by) % size) for i in range(size)])


def quantize(deltas, exponents):
    scales = jnp.where(exponents < 0, 0.5, jnp.where(exponents > 0, 2.0, 1.0)).astype(jnp.float32)
    blocked = deltas.reshape(exponents.shape[0], 32, exponents.shape[1])
    scaled = blocked / scales[:, None, :]
    magnitude = jnp.minimum(jnp.abs(scaled), 6.0)
    spacing = jnp.where(magnitude < 2.0, 0.5, jnp.where(magnitude < 4.0, 1.0, 2.0))
    levels = jnp.floor(magnitude / spacing + 0.5) * spacing
    signed = jnp.sign(scaled) * levels * scales[:, None, :]
    return signed.reshape(deltas.shape)


def project_keys(normed, weights):
    product = jnp.dot(normed, weights, preferred_element_type=jnp.float32)
    return (product * D ** (-0.5)).astype(jnp.bfloat16)


def shards(base_weights, local_weights, outer_momentum, scale_exponents, section_inputs, norm_gain):
    base_layer = base_weights[0]
    local_layer = local_weights[0, 0]
    base_f = base_layer.astype(jnp.float32)
    quantized = quantize(base_f - local_layer.astype(jnp.float32), scale_exponents[0])
    replicas = lax.axis_size("replica")
    moment = outer_momentum[0]
    row_count = moment.shape[0]
    first_own = lax.axis_index("replica") * row_count
    summed = lax.psum(quantized.astype(jnp.bfloat16), "replica").astype(jnp.float32)
    own_rows = lax.dynamic_slice_in_dim(summed, first_own, row_count, 0)
    moment_new = MOMENTUM_DECAY * moment + own_rows / replicas
    moment_all = lax.all_gather(moment_new, "replica", axis=0, tiled=True)
    pseudo = summed / replicas
    new_base = (base_f - OUTER_RATE * (pseudo + MOMENTUM_DECAY * moment_all)).astype(jnp.bfloat16)
    activations = section_inputs[0, 0]
    passed = passed_along(activations, "section", 1).astype(jnp.float32)
    meansq = jnp.mean(passed * passed, axis=-1, keepdims=True)
    normed = (passed * lax.rsqrt(meansq + NORM_EPSILON) * norm_gain[0][None, :]).astype(
        jnp.bfloat16
    )
    column_keys = project_keys(lax.all_gather(normed, "tensor", axis=0, tiled=True), local_layer)
    key_out = lax.all_to_all(column_keys, "tensor", split_axis=0, concat_axis=1, tiled=True)
    return (new_base[None], moment_new[None], key_out[None, None])


def solution(mesh):
    placed = (
        P("section", None, "tensor"),
        P("replica", "section", None, "tensor"),
        P("section", "replica", "tensor"),
        P("section", None, "tensor"),
        P("replica", "section", "tensor", None),
        P("section", None),
    )
    return jax.shard_map(
        shards,
        mesh=mesh,
        in_specs=placed,
        out_specs=(
            P("section", None, "tensor"),
            P("section", "replica", "tensor"),
            P("replica", "section", "tensor", None),
        ),
        check_vma=False,
    )
```

profile of v0, /device:TPU:24, one launch (start us, length us, event | category | flops | bytes accessed | tf_op | source)
XLA Modules:
  0.0 665.8 jit_solution(5565506138257644838)
XLA Ops:
  7.2 0.0 all-reduce.2.cloned.1.call-start
  7.2 1.0 select_bitcast_fusion
  8.2 10.4 %fusion.4 = bf16[8192,256]{1,0:T(8,128)(2,1)} fusion(bf16[1,1,8192,256]{3,2,1,0:T(8,128)(2,1)} %param.7, bf16[1,8192,256]{2,1,0:T(8,128)(2,1)} %param.6, f32[256,256]{1,0:T(8,128)S(1)} %select_bitcast_fusion), kind=kLoop, calls=%fused_computation.10 | loop fusion | flops 37748736 | bytes 12845056 | tf_op jit(solution)/shard_map/convert_element_type | solution.py:44
  18.6 0.0 all-reduce.2.cloned.1.call-update
  18.6 0.0 all-gather.3.cloned.1.call-start
  18.7 184.2 %all-reduce.2.cloned.1.call-done = bf16[8192,256]{1,0:T(8,128)(2,1)} async-done(((bf16[8192,256]{1,0:T(8,128)(2,1)}), bf16[8192,256]{1,0:T(8,128)(2,1)}) %all-reduce.2.cloned.1.call-update) | async-done | bytes 4194320 | tf_op jit(solution)/shard_map/psum | solution.py:44
  202.8 2.8 convert_element_type.35
  205.7 0.0 copy-done
  205.7 0.0 copy-start.1
  205.7 1.2 bitcast_add_fusion
  206.9 0.0 all-gather.3.cloned.1.call-update
  206.9 0.0 all-gather.5.cloned.1.call-start
  207.0 2.9 collective-permute-start
  209.9 382.0 %collective-permute-done = bf16[640,8192]{1,0:T(8,128)(2,1)S(1)} collective-permute-done((bf16[640,8192]{1,0:T(8,128)(2,1)}, bf16[640,8192]{1,0:T(8,128)(2,1)S(1)}, u32[]{:S(2)}, u32[]{:S(2)}) %collective-permute-start) | collective-permute-done | bytes 10485792 | tf_op jit(solution)/shard_map/ppermute | solution.py:16
  591.9 2.1 fusion
  594.1 5.7 fusion.2
  599.8 0.0 all-gather.5.cloned.1.call-update
  599.8 0.0 all-gather.3.cloned.1.call-done
  599.8 8.9 %fusion.6 = bf16[1,8192,256]{2,1,0:T(8,128)(2,1)} fusion(f32[8192,256]{1,0:T(8,128)} %all-gather.3.cloned.1.call-done, bf16[1,8192,256]{2,1,0:T(8,128)(2,1)} %param.6, bf16[8192,256]{1,0:T(8,128)(2,1)} %all-reduce.2.cloned.1.call-done), kind=kLoop, calls=%fused_computation.13 | loop fusion | flops 16777216 | bytes 20971520 | tf_op jit(solution)/shard_map/broadcast_in_dim | solution.py:58
  608.8 33.2 %all-gather.5.cloned.1.call-done = bf16[1280,8192]{1,0:T(8,128)(2,1)} async-done(((bf16[640,8192]{1,0:T(8,128)(2,1)}), bf16[1280,8192]{1,0:T(8,128)(2,1)}) %all-gather.5.cloned.1.call-update) | async-done | bytes 20971536 | tf_op jit(solution)/shard_map/all_gather | solution.py:56
  642.0 11.0 %fusion.12 = bf16[1280,256]{1,0:T(8,128)(2,1)S(1)} fusion(bf16[1280,8192]{1,0:T(8,128)(2,1)} %all-gather.5.cloned.1.call-done, bf16[1,1,8192,256]{3,2,1,0:T(8,128)(2,1)} %param.7), kind=kOutput, calls=%fused_computation.17 | convolution fusion | flops 5369364480 | bytes 25821184 | tf_op jit(solution)/shard_map/dot_general | solution.py:31
  653.0 4.3 all_to_all.16
  657.3 0.7 copy.9
  658.0 1.3 broadcast_in_dim.41
  (3 shorter events, 0.0 us)
Async XLA Ops:
  7.2 195.7 %all-reduce.2.cloned.1.call-start = ((), (), s32[]{:S(2)}) async-start(), calls=%async_computation.1 | async-start | bytes 8388608 | tf_op jit(solution)/shard_map/psum | solution.py:44
  18.6 187.1 %copy-start = (f32[1,1024,256]{2,1,0:T(8,128)S(1)}, f32[1,1024,256]{2,1,0:T(8,128)}, u32[]{:S(2)}) copy-start(f32[1,1024,256]{2,1,0:T(8,128)} %param.8) | copy-start | bytes 3145732
  18.6 581.2 %all-gather.3.cloned.1.call-start = ((), (), s32[]{:S(2)}) async-start(), calls=%async_computation.2 | async-start | bytes 9437184 | tf_op jit(solution)/shard_map/all_gather | solution.py:47
  205.7 388.4 %copy-start.1 = (f32[1,8192]{1,0:T(1,128)S(1)}, f32[1,8192]{1,0:T(1,128)}, u32[]{:S(2)}) copy-start(f32[1,8192]{1,0:T(1,128)} %param.11) | copy-start | bytes 98308
  206.9 435.1 %all-gather.5.cloned.1.call-start = ((), (), s32[]{:S(2)}) async-start(), calls=%async_computation.3 | async-start | bytes 31457280 | tf_op jit(solution)/shard_map/all_gather | solution.py:56
  207.0 385.0 %collective-permute-start = (bf16[640,8192]{1,0:T(8,128)(2,1)}, bf16[640,8192]{1,0:T(8,128)(2,1)S(1)}, u32[]{:S(2)}, u32[]{:S(2)}) collective-permute-start(bf16[640,8192]{1,0:T(8,128)(2,1)} %bitcast.35), channel_id=1, source_target_pairs={{0,2},{2,4},{4,6},{6,8},{8,10},{10,12},{12,14},{14,0},{1,3},{3,5},... | collective-permute-start | bytes 31457288 | tf_op jit(solution)/shard_map/ppermute | solution.py:16
Sparse Core Ops, SparseCore 0:
  18.7 184.0 all-reduce.1
  207.1 249.6 all-gather.2
  599.9 42.0 all-gather.4
where the time goes:
time: 667 us; the launch traced here: 666 us
  waiting for transfers between devices  599 us (90%)
  other arithmetic  32.2 us (5%)
  between operations  13.8 us (2%)
  matrix products  11 us (2%)
    ppermute x1, waiting for transfers between devices, passed_along(): lax.ppermute(shard, axis, [(i, (i + by) % size) for i in range(size)])  382 us
    psum x1, waiting for transfers between devices, shards(): lax.psum(quantized.astype(jnp.bfloat16), 'replica').astype(jnp.float32)  184 us
    all_gather x1, waiting for transfers between devices, shards(): lax.all_gather(normed, 'tensor', axis=0, tiled=True)  33.2 us
  transfers between devices with their start and end apart: 4, of which 3 were waited for; matrix products, arithmetic and copies ran while one was open for 3% of the time, Pallas kernels for 0%

commit v1 on v0

v1 whole, which is shorter than its diff:
```python
import jax
import jax.numpy as jnp
from jax import lax
from jax.experimental import pallas as pl
from jax.experimental.pallas import tpu as pltpu
from jax.sharding import PartitionSpec as P

MESH = pl.DeviceIdType.MESH
D = 8192
TOK = 640
KV = 256
LANES = 128
REPLICAS = 8
ROWS = D // REPLICAS
J = 4
JR = ROWS // J
NK = 8
KR = D // NK
NW = 2 * NK
XP = 4
XR = TOK // XP
NR = 32
MR = TOK // 2

OUTER_RATE = 0.7
MOMENTUM_DECAY = 0.9
NORM_EPSILON = 1e-05


def schedule():
    events = []
    for j in range(J):
        summed = 16 + 14 * j
        events += [(summed, "sum", j), (summed + 17, "update", j), (summed + 34, "pass", j)]
    events += [(14 + 7 * i, "weights", i) for i in range(NW)]
    return [(name, i) for _, name, i in sorted(events)]


def kernel(
    base, local, moment, exps, acts, gain,
    base_out, moment_out, keys_out,
    bbuf, qbuf, ebuf, mbuf, xbuf, gbuf, wbuf, rbuf, pbuf, zbuf, nbuf, acc, kbuf,
    load_b, load_q, load_e, load_m, load_x, store_n, store_m,
    g_send, g_recv, w_send, w_recv, f_send, f_recv, r_send, r_recv, z_send, z_recv,
    a_send, a_recv, o_send, o_recv, p_send, p_recv, k_send, k_recv,
):
    r, s, t = lax.axis_index("replica"), lax.axis_index("section"), lax.axis_index("tensor")
    x, zl = r // 2, r % 2
    before, after = (r, (s + 7) % 8, t), (r, (s + 1) % 8, t)
    sibling = (r, s, 1 - t)
    rz = x * 2 + 1 - zl
    pair = (rz, s, t)
    others = [(((x + d) % 4) * 2 + zl, s, t) for d in (1, 2, 3)]

    def rows(j):
        return pl.ds(j * JR, JR)

    def remote(src, dst, send, recv, to):
        return pltpu.make_async_remote_copy(
            src_ref=src, dst_ref=dst, send_sem=send, recv_sem=recv, device_id=to, device_id_type=MESH
        )

    def weights_copy(i):
        b, k = i // NK, i % NK
        cols = pl.ds(pl.multiple_of(b * LANES, LANES), LANES)
        deep = pl.ds(pl.multiple_of(k * KR, KR), KR)
        return remote(local.at[deep, cols], wbuf.at[b, t, deep], w_send.at[i], w_recv.at[i], before)

    def share_copy(i, core):
        b, k = i // NK, i % NK
        deep = pl.ds(pl.multiple_of(k * KR, KR), KR)
        ref = wbuf.at[b, core, deep]
        return remote(ref, ref, f_send.at[i], f_recv.at[i], sibling)

    gain_copy = remote(gain, gbuf, g_send, g_recv, before)

    def term_copy(j, d):
        xd = (x + d + 1) % 4
        return remote(
            qbuf.at[pl.ds(xd * 2, 2), rows(j)], rbuf.at[d, :, rows(j)],
            r_send.at[j, d], r_recv.at[j, d], others[d],
        )

    def half_copy(j):
        return remote(pbuf.at[1 - zl, rows(j)], zbuf.at[rows(j)], z_send.at[j], z_recv.at[j], pair)

    def pair_copy(j):
        return remote(nbuf.at[rows(j)], base_out.at[r, rows(j)], a_send.at[j], a_recv.at[j], pair)

    def own_copy(j, d):
        return remote(
            nbuf.at[rows(j)], base_out.at[r, rows(j)], o_send.at[j, d], o_recv.at[j, d], others[d]
        )

    def pass_copy(j, d):
        ref = base_out.at[rz, rows(j)]
        return remote(ref, ref, p_send.at[j, d], p_recv.at[j, d], others[d])

    def key_copy(b, c):
        return remote(
            kbuf.at[b, c], keys_out.at[:, pl.ds(c * KV + b * LANES, LANES)],
            k_send.at[b, c], k_recv.at[b, c], after,
        )

    def store_copy(j):
        return pltpu.make_async_copy(nbuf.at[rows(j)], base_out.at[r, rows(j)], store_n.at[j])

    store_moment = pltpu.make_async_copy(mbuf, moment_out, store_m)

    def load_base(j):
        return pltpu.make_async_copy(base.at[:, rows(j)], bbuf.at[:, rows(j)], load_b.at[j])

    local3 = local.reshape(REPLICAS, ROWS, KV)

    def load_local(j):
        return pltpu.make_async_copy(local3.at[:, rows(j)], qbuf.at[:, rows(j)], load_q.at[j])

    load_exps = pltpu.make_async_copy(exps, ebuf, load_e)
    load_moment = pltpu.make_async_copy(moment, mbuf, load_m)

    def load_acts(i):
        part = pl.ds(i * XR, XR)
        return pltpu.make_async_copy(acts.at[part], xbuf.at[part], load_x.at[i])

    load_exps.start()
    for j in range(J):
        load_base(j).start()
        load_local(j).start()
    for i in range(XP):
        load_acts(i).start()
    load_moment.start()

    barrier = pltpu.get_barrier_semaphore()
    for peer in (before, after, sibling, pair, *others):
        pl.semaphore_signal(barrier, inc=1, device_id=peer, device_id_type=MESH)
    pl.semaphore_wait(barrier, 7)

    gain_copy.start()

    @pl.loop(0, NW)
    def _(i):
        weights_copy(i).start()

    load_exps.wait()
    for j in range(J):
        load_base(j).wait()
        load_local(j).wait()

        @pl.loop(0, REPLICAS)
        def _(q):
            e = ebuf[q, pl.ds(j * (JR // 32), JR // 32), :]
            scale = jnp.where(e < 0, 0.5, jnp.where(e > 0, 2.0, 1.0)).astype(jnp.float32)
            inverse = jnp.where(e < 0, 2.0, jnp.where(e > 0, 0.5, 1.0)).astype(jnp.float32)
            delta = bbuf[q, rows(j), :].astype(jnp.float32) - qbuf[q, rows(j), :].astype(jnp.float32)
            y = delta.reshape(JR // 32, 32, KV) * inverse[:, None, :]
            a = jnp.minimum(jnp.abs(y), 6.0)
            spacing = jnp.where(a < 2.0, 0.5, jnp.where(a < 4.0, 1.0, 2.0))
            per = jnp.where(a < 2.0, 2.0, jnp.where(a < 4.0, 1.0, 0.5))
            level = jnp.floor(a * per + 0.5) * spacing * scale[:, None, :]
            level = jnp.where(y < 0.0, -level, level)
            qbuf[q, rows(j), :] = level.reshape(JR, KV).astype(jnp.bfloat16)

        for d in range(3):
            term_copy(j, d).start()

    for i in range(XP):
        load_acts(i).wait()
    gain_copy.wait_recv()

    @pl.loop(0, TOK // NR)
    def _(i):
        part = pl.ds(pl.multiple_of(i * NR, NR), NR)
        total = jnp.zeros((NR, LANES), jnp.float32)
        for k in range(NK):
            v = xbuf[part, k * KR : (k + 1) * KR].astype(jnp.float32)
            v = v * v
            for lane in range(0, KR, LANES):
                total = total + v[:, lane : lane + LANES]
        meansq = jnp.sum(total, axis=-1, keepdims=True) * (1.0 / D)
        factor = lax.rsqrt(meansq + NORM_EPSILON)
        for k in range(NK):
            cols = slice(k * KR, (k + 1) * KR)
            v = xbuf[part, cols].astype(jnp.float32)
            xbuf[part, cols] = (v * factor * gbuf[:, cols]).astype(jnp.bfloat16)

    load_moment.wait()

    def sum_terms(j):
        for d in range(3):
            term_copy(j, d).wait_recv()
        for h in range(2):
            total = qbuf[x * 2 + h, rows(j), :].astype(jnp.float32)
            for d in range(3):
                total = total + rbuf[d, h, rows(j), :].astype(jnp.float32)
            pbuf[h, rows(j), :] = total.astype(jnp.bfloat16)
        half_copy(j).start()

    def update(j):
        half_copy(j).wait_recv()
        total = pbuf[zl, rows(j), :].astype(jnp.float32) + zbuf[rows(j), :].astype(jnp.float32)
        pseudo = total * (1.0 / REPLICAS)
        new = MOMENTUM_DECAY * mbuf[rows(j), :] + pseudo
        mbuf[rows(j), :] = new
        old = bbuf[r, rows(j), :].astype(jnp.float32)
        nbuf[rows(j), :] = (old - OUTER_RATE * (pseudo + MOMENTUM_DECAY * new)).astype(jnp.bfloat16)
        pair_copy(j).start()
        for d in range(3):
            own_copy(j, d).start()
        store_copy(j).start()
        if j == J - 1:
            store_moment.start()

    def pass_on(j):
        pair_copy(j).wait_recv()
        for d in range(3):
            pass_copy(j, d).start()

    def weights(i):
        weights_copy(i).wait_recv()
        share_copy(i, t).start()

    def multiply(first, last):
        @pl.loop(first, last)
        def _(i):
            weights(i)
            share_copy(i, 1 - t).wait_recv()
            b, k = i // NK, i % NK
            deep = pl.ds(pl.multiple_of(k * KR, KR), KR)

            @pl.loop(0, TOK // MR)
            def _(m):
                part = pl.ds(pl.multiple_of(m * MR, MR), MR)
                w = jnp.concatenate([wbuf[b, 0, deep, :], wbuf[b, 1, deep, :]], axis=1)
                product = jnp.dot(xbuf[part, deep], w, preferred_element_type=jnp.float32)
                kept = jnp.where(k == 0, 0.0, acc[part, :])
                acc[part, :] = kept + product

    def keys(b):
        for c in range(2):
            kbuf[b, c] = (acc[:, c * LANES : (c + 1) * LANES] * D ** (-0.5)).astype(jnp.bfloat16)
            key_copy(b, c).start()

    run = []

    def flush():
        if run:
            multiply(run[0], run[-1] + 1)
            if run[-1] % NK == NK - 1:
                keys(run[-1] // NK)
            run.clear()

    for name, i in schedule():
        if name == "weights":
            run.append(i)
            if i % NK == NK - 1:
                flush()
            continue
        flush()
        {"sum": sum_terms, "update": update, "pass": pass_on}[name](i)
    flush()

    gain_copy.wait_send()

    @pl.loop(0, NW)
    def _(i):
        weights_copy(i).wait_send()
        share_copy(i, t).wait_send()

    @pl.loop(0, J)
    def _(j):
        half_copy(j).wait_send()
        pair_copy(j).wait_send()
        store_copy(j).wait()
        for d in range(3):
            term_copy(j, d).wait_send()
            own_copy(j, d).wait()
            pass_copy(j, d).wait()

    store_moment.wait()
    for b in range(2):
        for c in range(2):
            key_copy(b, c).wait()


def shards(base_weights, local_weights, outer_momentum, scale_exponents, section_inputs, norm_gain):
    bf16, f32 = jnp.bfloat16, jnp.float32
    hbm = pl.BlockSpec(memory_space=pl.ANY)
    dma = pltpu.SemaphoreType.DMA
    new_base, new_moment, keys = pl.pallas_call(
        kernel,
        out_shape=(
            jax.ShapeDtypeStruct((REPLICAS, ROWS, KV), bf16),
            jax.ShapeDtypeStruct((ROWS, KV), f32),
            jax.ShapeDtypeStruct((TOK, 2 * KV), bf16),
        ),
        in_specs=[hbm] * 6,
        out_specs=(hbm, hbm, hbm),
        scratch_shapes=[
            pltpu.VMEM((REPLICAS, ROWS, KV), bf16),
            pltpu.VMEM((REPLICAS, ROWS, KV), bf16),
            pltpu.VMEM((REPLICAS, ROWS // 32, KV), jnp.int32),
            pltpu.VMEM((ROWS, KV), f32),
            pltpu.VMEM((TOK, D), bf16),
            pltpu.VMEM((1, D), f32),
            pltpu.VMEM((2, 2, D, LANES), bf16),
            pltpu.VMEM((3, 2, ROWS, KV), bf16),
            pltpu.VMEM((2, ROWS, KV), bf16),
            pltpu.VMEM((ROWS, KV), bf16),
            pltpu.VMEM((ROWS, KV), bf16),
            pltpu.VMEM((TOK, KV), f32),
            pltpu.VMEM((2, 2, TOK, LANES), bf16),
            dma((J,)), dma((J,)), dma, dma, dma((XP,)), dma((J,)), dma,
            dma, dma, dma((NW,)), dma((NW,)), dma((NW,)), dma((NW,)),
            dma((J, 3)), dma((J, 3)), dma((J,)), dma((J,)),
            dma((J,)), dma((J,)), dma((J, 3)), dma((J, 3)), dma((J, 3)), dma((J, 3)),
            dma((2, 2)), dma((2, 2)),
        ],
        compiler_params=pltpu.CompilerParams(
            collective_id=0, has_side_effects=True, vmem_limit_bytes=56 << 20
        ),
        cost_estimate=pl.CostEstimate(
            flops=2 * TOK * D * 2 * KV, bytes_accessed=40 << 20, transcendentals=0
        ),
    )(
        base_weights.reshape(REPLICAS, ROWS, KV),
        local_weights.reshape(D, KV),
        outer_momentum.reshape(ROWS, KV),
        scale_exponents.reshape(REPLICAS, ROWS // 32, KV),
        section_inputs.reshape(TOK, D),
        norm_gain,
    )
    return (
        new_base.reshape(1, D, KV),
        new_moment.reshape(1, ROWS, KV),
        keys.reshape(1, 1, TOK, 2 * KV),
    )


def solution(mesh):
    placed = (
        P("section", None, "tensor"),
        P("replica", "section", None, "tensor"),
        P("section", "replica", "tensor"),
        P("section", None, "tensor"),
        P("replica", "section", "tensor", None),
        P("section", None),
    )
    return jax.shard_map(
        shards,
        mesh=mesh,
        in_specs=placed,
        out_specs=(
            P("section", None, "tensor"),
            P("section", "replica", "tensor"),
            P("replica", "section", "tensor", None),
        ),
        check_vma=False,
    )
```

time: 667 us -> 159 us (0.24)
  waiting for transfers between devices: 599 us -> 0 us
  Pallas kernels: 0 us -> 152 us
  other arithmetic: 32.2 us -> 0 us
  between operations: 13.8 us -> 0.66 us
  matrix products: 11 us -> 0 us
    ppermute x1 -> x0, waiting for transfers between devices: 382 us -> none  [passed_along(): lax.ppermute(shard, axis, [(i, (i + by) % size) for i in range(size)])]
    psum x1 -> x0, waiting for transfers between devices: 184 us -> none  [shards(): lax.psum(quantized.astype(jnp.bfloat16), 'replica').astype(jnp.float32)]
    pallas_call x0 -> x1, Pallas kernels: none -> 152 us  [shards(): pl.pallas_call(kernel, out_shape=(jax.ShapeDtypeStruct((REPLICAS, ROWS, K...]
    all_gather x2 -> x0, waiting for transfers between devices: 33.2 us -> none  [the longest x1 33.2 us: shards(): lax.all_gather(normed, 'tensor', axis=0, tiled=True)]
    convert_element_type x3 -> x0, other arithmetic: 18.9 us -> none  [the longest x1 10.4 us: shards(): quantized.astype(jnp.bfloat16)]
    dot_general x1 -> x0, matrix products: 11 us -> none  [project_keys(): product = jnp.dot(normed, weights, preferred_element_type=jnp.float32)]
    broadcast_in_dim x1 -> x0, other arithmetic: 8.93 us -> none  [shards(): return (new_base[None], moment_new[None], key_out[None, None])]
  transfers between devices with their start and end apart: 4 -> 0, of which waited for: 3 -> 0; matrix products, arithmetic and copies ran while one was open for 3% -> 0% of each run, Pallas kernels for 0% -> 0%
where the time goes in v1:
time: 159 us
  Pallas kernels  152 us (96%)
  local copies, waits for them, and re-layouts  6.41 us (4%)
    pallas_call x1, Pallas kernels, shards(): pl.pallas_call(kernel, out_shape=(jax.ShapeDtypeStruct((REPLICAS, ROWS, K...  152 us
    unnamed x7, local copies, waits for them, and re-layouts  6.41 us

profile of v1, /device:TPU:24, one launch (start us, length us, event | category | flops | bytes accessed | tf_op | source)
XLA Modules:
  0.0 159.2 jit_solution(14954404811162362105)
XLA Ops:
  0.6 152.1 %shard_map.85 = (bf16[8,1024,256]{2,1,0:T(8,128)(2,1)}, f32[1024,256]{1,0:T(8,128)}, bf16[640,512]{1,0:T(8,128)(2,1)}) custom-call(bf16[8,1024,256]{2,1,0:T(8,128)(2,1)} %bitcast.9, bf16[8192,256]{1,0:T(8,128)(2,1)} %bitcast.10, f32[1024,256]{1,0:T(8,128)} %bitcast.12, s32[8,32,256]{2,1,0:T(8,128)} %bitcast.15, bf16[640,8192]{1,0:T(8,128)(2,1)} %bitcast.8, ...), custom_call_target="tpu_custom_call" | custom-call | flops 5368709120 | bytes 41943040 | tf_op jit(solution)/shard_map/pallas_call | solution.py:289
  152.7 0.0 copy-start
  152.7 0.0 copy-start.1
  152.8 4.6 %copy.12 = bf16[1,8192,256]{2,1,0:T(8,128)(2,1)} copy(bf16[1,8192,256]{2,1,0:T(8,128)(2,1)} %bitcast.11) | data formatting | bytes 8388608
  157.3 0.0 copy-done
  157.4 1.0 copy.13
  158.3 0.0 copy-done.1
  158.3 0.8 copy.14
Async XLA Ops:
  152.7 4.6 %copy-start = (f32[1024,256]{1,0:T(8,128)S(1)}, f32[1024,256]{1,0:T(8,128)}, u32[]{:S(2)}) copy-start(f32[1024,256]{1,0:T(8,128)} %get-tuple-element.7) | copy-start | bytes 3145732
  152.7 5.6 %copy-start.1 = (bf16[640,512]{1,0:T(8,128)(2,1)S(1)}, bf16[640,512]{1,0:T(8,128)(2,1)}, u32[]{:S(2)}) copy-start(bf16[640,512]{1,0:T(8,128)(2,1)} %get-tuple-element.8) | copy-start | bytes 1966084

commit v2 on v1

--- a/solution.py
+++ b/solution.py
@@ -27,22 +27,30 @@
 NORM_EPSILON = 1e-05
 
 
-def schedule():
-    events = []
-    for j in range(J):
-        summed = 16 + 14 * j
-        events += [(summed, "sum", j), (summed + 17, "update", j), (summed + 34, "pass", j)]
-    events += [(14 + 7 * i, "weights", i) for i in range(NW)]
-    return [(name, i) for _, name, i in sorted(events)]
+EARLY = 10
+ORDER = (
+    [("relay", 0), ("normalize", 0), ("normalize", 1), ("sum", 0), ("normalize", 2), ("normalize", 3)]
+    + [("relay", 1), ("sum", 1), ("weights", 0), ("weights", 1)]
+    + [("relay", 2), ("sum", 2), ("weights", 2), ("weights", 3), ("relay", 3), ("sum", 3)]
+    + [("send", i) for i in range(EARLY, 13)]
+    + [("weights", i) for i in range(4, 8)]
+    + [("update", j) for j in range(J)]
+    + [("send", i) for i in range(13, NW)]
+    + [("hop", j) for j in range(J)]
+    + [("weights", i) for i in range(8, 11)]
+    + [("pass", j) for j in range(J)]
+    + [("hop_pair", j) for j in range(J)]
+    + [("weights", i) for i in range(11, NW)]
+)
 
 
 def kernel(
     base, local, moment, exps, acts, gain,
     base_out, moment_out, keys_out,
-    bbuf, qbuf, ebuf, mbuf, xbuf, gbuf, wbuf, rbuf, pbuf, zbuf, nbuf, acc, kbuf,
+    bbuf, qbuf, ebuf, mbuf, xbuf, gbuf, wbuf, vbuf, sbuf, dbuf, pbuf, zbuf, nbuf, acc, kbuf,
     load_b, load_q, load_e, load_m, load_x, store_n, store_m,
-    g_send, g_recv, w_send, w_recv, f_send, f_recv, r_send, r_recv, z_send, z_recv,
-    a_send, a_recv, o_send, o_recv, p_send, p_recv, k_send, k_recv,
+    g_send, g_recv, w_send, w_recv, f_send, f_recv, v_send, v_recv, s_send, s_recv, d_send, d_recv,
+    z_send, z_recv, a_send, a_recv, n_send, n_recv, h_send, h_recv, k_send, k_recv,
 ):
     r, s, t = lax.axis_index("replica"), lax.axis_index("section"), lax.axis_index("tensor")
     x, zl = r // 2, r % 2
@@ -50,7 +58,8 @@
     sibling = (r, s, 1 - t)
     rz = x * 2 + 1 - zl
     pair = (rz, s, t)
-    others = [(((x + d) % 4) * 2 + zl, s, t) for d in (1, 2, 3)]
+    up, down = ((x + 1) % 4) * 2 + zl, ((x + 3) % 4) * 2 + zl
+    along = [(up, s, t), (down, s, t)]
 
     def rows(j):
         return pl.ds(j * JR, JR)
@@ -74,11 +83,21 @@
 
     gain_copy = remote(gain, gbuf, g_send, g_recv, before)
 
-    def term_copy(j, d):
-        xd = (x + d + 1) % 4
+    def shard(d):
+        return (x + d) % 4 * 2
+
+    def via_copy(j, h):
         return remote(
-            qbuf.at[pl.ds(xd * 2, 2), rows(j)], rbuf.at[d, :, rows(j)],
-            r_send.at[j, d], r_recv.at[j, d], others[d],
+            qbuf.at[shard(2) + h, rows(j)], vbuf.at[h, rows(j)], v_send.at[h, j], v_recv.at[h, j], along[h]
+        )
+
+    def sum_copy(j, h):
+        return remote(vbuf.at[h, rows(j)], sbuf.at[h, rows(j)], s_send.at[h, j], s_recv.at[h, j], along[h])
+
+    def term_copy(j, h):
+        return remote(
+            qbuf.at[shard(3 if h == 0 else 1) + h, rows(j)], dbuf.at[h, rows(j)],
+            d_send.at[h, j], d_recv.at[h, j], along[1 - h],
         )
 
     def half_copy(j):
@@ -87,14 +106,23 @@
     def pair_copy(j):
         return remote(nbuf.at[rows(j)], base_out.at[r, rows(j)], a_send.at[j], a_recv.at[j], pair)
 
-    def own_copy(j, d):
+    def own_copy(j, w):
         return remote(
-            nbuf.at[rows(j)], base_out.at[r, rows(j)], o_send.at[j, d], o_recv.at[j, d], others[d]
+            nbuf.at[rows(j)], base_out.at[r, rows(j)], n_send.at[zl, w, j], n_recv.at[zl, w, j], along[w]
         )
 
-    def pass_copy(j, d):
+    def pass_copy(j, w):
         ref = base_out.at[rz, rows(j)]
-        return remote(ref, ref, p_send.at[j, d], p_recv.at[j, d], others[d])
+        return remote(ref, ref, n_send.at[1 - zl, w, j], n_recv.at[1 - zl, w, j], along[w])
+
+    def came_copy(j, h, w):
+        ref = base_out.at[(x + 3 + 2 * w) % 4 * 2 + h, rows(j)]
+        return remote(ref, ref, n_send.at[h, w, j], n_recv.at[h, w, j], along[0])
+
+    def hop_copy(j, h):
+        ref = base_out.at[(x + 3 + 2 * h) % 4 * 2 + h, rows(j)]
+        to = ((x + 1 + 2 * h) % 4 * 2 + zl, s, t)
+        return remote(ref, ref, h_send.at[h, j], h_recv.at[h, j], to)
 
     def key_copy(b, c):
         return remote(
@@ -126,18 +154,15 @@
     for j in range(J):
         load_base(j).start()
         load_local(j).start()
-    for i in range(XP):
-        load_acts(i).start()
-    load_moment.start()
 
     barrier = pltpu.get_barrier_semaphore()
-    for peer in (before, after, sibling, pair, *others):
+    for peer in (before, after, sibling, pair, *along):
         pl.semaphore_signal(barrier, inc=1, device_id=peer, device_id_type=MESH)
-    pl.semaphore_wait(barrier, 7)
+    pl.semaphore_wait(barrier, 6)
 
     gain_copy.start()
 
-    @pl.loop(0, NW)
+    @pl.loop(0, EARLY)
     def _(i):
         weights_copy(i).start()
 
@@ -160,42 +185,55 @@
             level = jnp.where(y < 0.0, -level, level)
             qbuf[q, rows(j), :] = level.reshape(JR, KV).astype(jnp.bfloat16)
 
-        for d in range(3):
-            term_copy(j, d).start()
-
-    for i in range(XP):
-        load_acts(i).wait()
-    gain_copy.wait_recv()
-
-    @pl.loop(0, TOK // NR)
-    def _(i):
-        part = pl.ds(pl.multiple_of(i * NR, NR), NR)
-        total = jnp.zeros((NR, LANES), jnp.float32)
-        for k in range(NK):
-            v = xbuf[part, k * KR : (k + 1) * KR].astype(jnp.float32)
-            v = v * v
-            for lane in range(0, KR, LANES):
-                total = total + v[:, lane : lane + LANES]
-        meansq = jnp.sum(total, axis=-1, keepdims=True) * (1.0 / D)
-        factor = lax.rsqrt(meansq + NORM_EPSILON)
-        for k in range(NK):
-            cols = slice(k * KR, (k + 1) * KR)
-            v = xbuf[part, cols].astype(jnp.float32)
-            xbuf[part, cols] = (v * factor * gbuf[:, cols]).astype(jnp.bfloat16)
-
-    load_moment.wait()
+        for h in range(2):
+            via_copy(j, h).start()
+        for h in range(2):
+            term_copy(j, h).start()
+        if j == 1:
+            for i in range(XP):
+                load_acts(i).start()
+            load_moment.start()
+
+    def normalize(part_at):
+        load_acts(part_at).wait()
+        if part_at == 0:
+            gain_copy.wait_recv()
+
+        @pl.loop(0, XR // NR)
+        def _(i):
+            part = pl.ds(pl.multiple_of(part_at * XR + i * NR, NR), NR)
+            total = jnp.zeros((NR, LANES), jnp.float32)
+            for k in range(NK):
+                v = xbuf[part, k * KR : (k + 1) * KR].astype(jnp.float32)
+                v = v * v
+                for lane in range(0, KR, LANES):
+                    total = total + v[:, lane : lane + LANES]
+            meansq = jnp.sum(total, axis=-1, keepdims=True) * (1.0 / D)
+            factor = lax.rsqrt(meansq + NORM_EPSILON)
+            for k in range(NK):
+                cols = slice(k * KR, (k + 1) * KR)
+                v = xbuf[part, cols].astype(jnp.float32)
+                xbuf[part, cols] = (v * factor * gbuf[:, cols]).astype(jnp.bfloat16)
+
+    def relay(j):
+        for h in range(2):
+            via_copy(j, h).wait_recv()
+            mine = qbuf[shard(1 if h == 0 else 3) + h, rows(j), :].astype(jnp.float32)
+            vbuf[h, rows(j), :] = (vbuf[h, rows(j), :].astype(jnp.float32) + mine).astype(jnp.bfloat16)
+            sum_copy(j, h).start()
 
     def sum_terms(j):
-        for d in range(3):
-            term_copy(j, d).wait_recv()
         for h in range(2):
+            term_copy(j, h).wait_recv()
+            sum_copy(j, h).wait_recv()
             total = qbuf[x * 2 + h, rows(j), :].astype(jnp.float32)
-            for d in range(3):
-                total = total + rbuf[d, h, rows(j), :].astype(jnp.float32)
+            total = total + sbuf[h, rows(j), :].astype(jnp.float32) + dbuf[h, rows(j), :].astype(jnp.float32)
             pbuf[h, rows(j), :] = total.astype(jnp.bfloat16)
         half_copy(j).start()
 
     def update(j):
+        if j == 0:
+            load_moment.wait()
         half_copy(j).wait_recv()
         total = pbuf[zl, rows(j), :].astype(jnp.float32) + zbuf[rows(j), :].astype(jnp.float32)
         pseudo = total * (1.0 / REPLICAS)
@@ -204,36 +242,47 @@
         old = bbuf[r, rows(j), :].astype(jnp.float32)
         nbuf[rows(j), :] = (old - OUTER_RATE * (pseudo + MOMENTUM_DECAY * new)).astype(jnp.bfloat16)
         pair_copy(j).start()
-        for d in range(3):
-            own_copy(j, d).start()
+        for w in range(2):
+            own_copy(j, w).start()
         store_copy(j).start()
         if j == J - 1:
             store_moment.start()
 
     def pass_on(j):
         pair_copy(j).wait_recv()
-        for d in range(3):
-            pass_copy(j, d).start()
+        for w in range(2):
+            pass_copy(j, w).start()
+
+    def hop(j, h):
+        came_copy(j, h, h).wait_recv()
+        hop_copy(j, h).start()
 
     def weights(i):
         weights_copy(i).wait_recv()
         share_copy(i, t).start()
 
-    def multiply(first, last):
+    def multiply(i):
+        share_copy(i, 1 - t).wait_recv()
+        b, k = i // NK, i % NK
+        deep = pl.ds(pl.multiple_of(k * KR, KR), KR)
+
+        @pl.loop(0, TOK // MR)
+        def _(m):
+            part = pl.ds(pl.multiple_of(m * MR, MR), MR)
+            w = jnp.concatenate([wbuf[b, 0, deep, :], wbuf[b, 1, deep, :]], axis=1)
+            product = jnp.dot(xbuf[part, deep], w, preferred_element_type=jnp.float32)
+            kept = jnp.where(k == 0, 0.0, acc[part, :])
+            acc[part, :] = kept + product
+
+    def arrive(first, last):
+        if first == 0:
+            weights(0)
+            first = 1
+
         @pl.loop(first, last)
         def _(i):
             weights(i)
-            share_copy(i, 1 - t).wait_recv()
-            b, k = i // NK, i % NK
-            deep = pl.ds(pl.multiple_of(k * KR, KR), KR)
-
-            @pl.loop(0, TOK // MR)
-            def _(m):
-                part = pl.ds(pl.multiple_of(m * MR, MR), MR)
-                w = jnp.concatenate([wbuf[b, 0, deep, :], wbuf[b, 1, deep, :]], axis=1)
-                product = jnp.dot(xbuf[part, deep], w, preferred_element_type=jnp.float32)
-                kept = jnp.where(k == 0, 0.0, acc[part, :])
-                acc[part, :] = kept + product
+            multiply(i - 1)
 
     def keys(b):
         for c in range(2):
@@ -244,20 +293,29 @@
 
     def flush():
         if run:
-            multiply(run[0], run[-1] + 1)
-            if run[-1] % NK == NK - 1:
-                keys(run[-1] // NK)
+            arrive(run[0], run[-1] + 1)
+            if run[-1] == NK:
+                keys(0)
             run.clear()
 
-    for name, i in schedule():
+    for name, i in ORDER:
         if name == "weights":
             run.append(i)
-            if i % NK == NK - 1:
+            if i == NK:
                 flush()
             continue
         flush()
-        {"sum": sum_terms, "update": update, "pass": pass_on}[name](i)
+        if name == "send":
+            weights_copy(i).start()
+        elif name == "hop":
+            hop(i, zl)
+        elif name == "hop_pair":
+            hop(i, 1 - zl)
+        else:
+            {"normalize": normalize, "relay": relay, "sum": sum_terms, "update": update, "pass": pass_on}[name](i)
     flush()
+    multiply(NW - 1)
+    keys(1)
 
     gain_copy.wait_send()
 
@@ -271,10 +329,14 @@
         half_copy(j).wait_send()
         pair_copy(j).wait_send()
         store_copy(j).wait()
-        for d in range(3):
-            term_copy(j, d).wait_send()
-            own_copy(j, d).wait()
-            pass_copy(j, d).wait()
+        for h in range(2):
+            via_copy(j, h).wait_send()
+            sum_copy(j, h).wait_send()
+            term_copy(j, h).wait_send()
+            own_copy(j, h).wait_send()
+            pass_copy(j, h).wait_send()
+            came_copy(j, h, 1 - h).wait_recv()
+            hop_copy(j, h).wait()
 
     store_moment.wait()
     for b in range(2):
@@ -303,7 +365,9 @@
             pltpu.VMEM((TOK, D), bf16),
             pltpu.VMEM((1, D), f32),
             pltpu.VMEM((2, 2, D, LANES), bf16),
-            pltpu.VMEM((3, 2, ROWS, KV), bf16),
+            pltpu.VMEM((2, ROWS, KV), bf16),
+            pltpu.VMEM((2, ROWS, KV), bf16),
+            pltpu.VMEM((2, ROWS, KV), bf16),
             pltpu.VMEM((2, ROWS, KV), bf16),
             pltpu.VMEM((ROWS, KV), bf16),
             pltpu.VMEM((ROWS, KV), bf16),
@@ -311,8 +375,8 @@
             pltpu.VMEM((2, 2, TOK, LANES), bf16),
             dma((J,)), dma((J,)), dma, dma, dma((XP,)), dma((J,)), dma,
             dma, dma, dma((NW,)), dma((NW,)), dma((NW,)), dma((NW,)),
-            dma((J, 3)), dma((J, 3)), dma((J,)), dma((J,)),
-            dma((J,)), dma((J,)), dma((J, 3)), dma((J, 3)), dma((J, 3)), dma((J, 3)),
+            dma((2, J)), dma((2, J)), dma((2, J)), dma((2, J)), dma((2, J)), dma((2, J)),
+            dma((J,)), dma((J,)), dma((J,)), dma((J,)), dma((2, 2, J)), dma((2, 2, J)), dma((2, J)), dma((2, J)),
             dma((2, 2)), dma((2, 2)),
         ],
         compiler_params=pltpu.CompilerParams(

time: 159 us -> 153 us (0.962)
  Pallas kernels: 152 us -> 146 us
    pallas_call x1, Pallas kernels: 152 us -> 146 us  [shards(): pl.pallas_call(kernel, out_shape=(jax.ShapeDtypeStruct((REPLICAS, ROWS, K...]
where the time goes in v2:
time: 153 us
  Pallas kernels  146 us (95%)
  local copies, waits for them, and re-layouts  6.41 us (4%)
    pallas_call x1, Pallas kernels, shards(): pl.pallas_call(kernel, out_shape=(jax.ShapeDtypeStruct((REPLICAS, ROWS, K...  146 us
    unnamed x7, local copies, waits for them, and re-layouts  6.41 us

profile of v2, /device:TPU:24, one launch (start us, length us, event | category | flops | bytes accessed | tf_op | source)
XLA Modules:
  0.0 152.7 jit_solution(11643362309386228021)
XLA Ops:
  0.6 145.7 %shard_map.85 = (bf16[8,1024,256]{2,1,0:T(8,128)(2,1)}, f32[1024,256]{1,0:T(8,128)}, bf16[640,512]{1,0:T(8,128)(2,1)}) custom-call(bf16[8,1024,256]{2,1,0:T(8,128)(2,1)} %bitcast.9, bf16[8192,256]{1,0:T(8,128)(2,1)} %bitcast.10, f32[1024,256]{1,0:T(8,128)} %bitcast.12, s32[8,32,256]{2,1,0:T(8,128)} %bitcast.15, bf16[640,8192]{1,0:T(8,128)(2,1)} %bitcast.8, ...), custom_call_target="tpu_custom_call" | custom-call | flops 5368709120 | bytes 41943040 | tf_op jit(solution)/shard_map/pallas_call | solution.py:351
  146.3 0.0 copy-start
  146.3 0.0 copy-start.1
  146.3 4.6 %copy.12 = bf16[1,8192,256]{2,1,0:T(8,128)(2,1)} copy(bf16[1,8192,256]{2,1,0:T(8,128)(2,1)} %bitcast.11) | data formatting | bytes 8388608
  150.9 0.0 copy-done
  150.9 1.0 copy.13
  151.9 0.0 copy-done.1
  151.9 0.8 copy.14
Async XLA Ops:
  146.3 4.6 %copy-start = (f32[1024,256]{1,0:T(8,128)S(1)}, f32[1024,256]{1,0:T(8,128)}, u32[]{:S(2)}) copy-start(f32[1024,256]{1,0:T(8,128)} %get-tuple-element.7) | copy-start | bytes 3145732
  146.3 5.6 %copy-start.1 = (bf16[640,512]{1,0:T(8,128)(2,1)S(1)}, bf16[640,512]{1,0:T(8,128)(2,1)}, u32[]{:S(2)}) copy-start(bf16[640,512]{1,0:T(8,128)(2,1)} %get-tuple-element.8) | copy-start | bytes 1966084

commit v3 on v2

--- a/solution.py
+++ b/solution.py
@@ -27,20 +27,18 @@
 NORM_EPSILON = 1e-05
 
 
-EARLY = 10
+EARLY = 8
 ORDER = (
     [("relay", 0), ("normalize", 0), ("normalize", 1), ("sum", 0), ("normalize", 2), ("normalize", 3)]
     + [("relay", 1), ("sum", 1), ("weights", 0), ("weights", 1)]
     + [("relay", 2), ("sum", 2), ("weights", 2), ("weights", 3), ("relay", 3), ("sum", 3)]
-    + [("send", i) for i in range(EARLY, 13)]
-    + [("weights", i) for i in range(4, 8)]
+    + [("weights", i) for i in range(4, NK)]
     + [("update", j) for j in range(J)]
-    + [("send", i) for i in range(13, NW)]
-    + [("hop", j) for j in range(J)]
-    + [("weights", i) for i in range(8, 11)]
+    + [("odd rest", 0), ("keys", 0), ("hop", 0), ("hop", 1)]
     + [("pass", j) for j in range(J)]
+    + [("even rest", 0), ("hop", 2), ("hop", 3)]
     + [("hop_pair", j) for j in range(J)]
-    + [("weights", i) for i in range(11, NW)]
+    + [("weights", i) for i in range(NK, NW)]
 )
 
 
@@ -275,9 +273,9 @@
             acc[part, :] = kept + product
 
     def arrive(first, last):
-        if first == 0:
-            weights(0)
-            first = 1
+        if first % NK == 0:
+            weights(first)
+            first += 1
 
         @pl.loop(first, last)
         def _(i):
@@ -294,19 +292,26 @@
     def flush():
         if run:
             arrive(run[0], run[-1] + 1)
-            if run[-1] == NK:
-                keys(0)
             run.clear()
 
     for name, i in ORDER:
         if name == "weights":
             run.append(i)
-            if i == NK:
+            if i % NK == NK - 1:
                 flush()
             continue
         flush()
-        if name == "send":
-            weights_copy(i).start()
+        if name in ("odd rest", "even rest"):
+
+            @pl.when(s % 2 == (1 if name == "odd rest" else 0))
+            def _():
+                @pl.loop(EARLY, NW)
+                def _(k):
+                    weights_copy(k).start()
+
+        elif name == "keys":
+            multiply(NK - 1)
+            keys(0)
         elif name == "hop":
             hop(i, zl)
         elif name == "hop_pair":
@@ -342,6 +347,23 @@
     for b in range(2):
         for c in range(2):
             key_copy(b, c).wait()
+
+
+def hand_on(base, moment, keys, base_out, moment_out, keys_out, base_held, moment_held, keys_held, came, left):
+    parts = [(base.at[i], base_held.at[i], base_out.at[i]) for i in range(REPLICAS)]
+    for i in range(2):
+        part = pl.ds(i * (ROWS // 2), ROWS // 2)
+        parts.append((moment.at[part], moment_held.at[part], moment_out.at[part]))
+    parts.append((keys, keys_held, keys_out))
+    reads = [pltpu.make_async_copy(src, held, came.at[i]) for i, (src, held, _) in enumerate(parts)]
+    writes = [pltpu.make_async_copy(held, dst, left.at[i]) for i, (_, held, dst) in enumerate(parts)]
+    for read in reads:
+        read.start()
+    for read, write in zip(reads, writes):
+        read.wait()
+        write.start()
+    for write in writes:
+        write.wait()
 
 
 def shards(base_weights, local_weights, outer_momentum, scale_exponents, section_inputs, norm_gain):
@@ -393,6 +415,16 @@
         section_inputs.reshape(TOK, D),
         norm_gain,
     )
+    outs = (new_base, new_moment, keys)
+    new_base, new_moment, keys = pl.pallas_call(
+        hand_on,
+        out_shape=tuple(jax.ShapeDtypeStruct(out.shape, out.dtype) for out in outs),
+        in_specs=[hbm] * 3,
+        out_specs=(hbm,) * 3,
+        scratch_shapes=[pltpu.VMEM(out.shape, out.dtype) for out in outs] + [dma((REPLICAS + 3,))] * 2,
+        compiler_params=pltpu.CompilerParams(vmem_limit_bytes=60 << 20),
+        cost_estimate=pl.CostEstimate(flops=0, bytes_accessed=12 << 20, transcendentals=0),
+    )(*outs)
     return (
         new_base.reshape(1, D, KV),
         new_moment.reshape(1, ROWS, KV),

time: 153 us -> 146 us (0.954)
  local copies, waits for them, and re-layouts: 6.41 us -> 0 us
  Pallas kernels: 146 us -> 144 us
    pallas_call x1, Pallas kernels: 146 us -> 139 us  [shards(): pl.pallas_call(kernel, out_shape=(jax.ShapeDtypeStruct((REPLICAS, ROWS, K...]
    unnamed x7 -> x0, local copies, waits for them, and re-layouts: 6.41 us -> none
    pallas_call x0 -> x1, Pallas kernels: none -> 5.34 us  [shards(): pl.pallas_call(hand_on, out_shape=tuple((jax.ShapeDtypeStruct(out.shape,...]
where the time goes in v3:
time: 146 us; the launch traced here: 145 us
  Pallas kernels  144 us (99%)
    pallas_call x1, Pallas kernels, shards(): pl.pallas_call(kernel, out_shape=(jax.ShapeDtypeStruct((REPLICAS, ROWS, K...  139 us
    pallas_call x1, Pallas kernels, shards(): pl.pallas_call(hand_on, out_shape=tuple((jax.ShapeDtypeStruct(out.shape,...  5.34 us

profile of v3, /device:TPU:24, one launch (start us, length us, event | category | flops | bytes accessed | tf_op | source)
XLA Modules:
  0.0 144.6 jit_solution(299726585092001967)
XLA Ops:
  0.6 138.6 %shard_map.85 = (bf16[8,1024,256]{2,1,0:T(8,128)(2,1)}, f32[1024,256]{1,0:T(8,128)}, bf16[640,512]{1,0:T(8,128)(2,1)}) custom-call(bf16[8,1024,256]{2,1,0:T(8,128)(2,1)} %bitcast.9, bf16[8192,256]{1,0:T(8,128)(2,1)} %bitcast.10, f32[1024,256]{1,0:T(8,128)} %bitcast.11, s32[8,32,256]{2,1,0:T(8,128)} %bitcast.12, bf16[640,8192]{1,0:T(8,128)(2,1)} %bitcast.8, ...), custom_call_target="tpu_custom_call" | custom-call | flops 5368709120 | bytes 41943040 | tf_op jit(solution)/shard_map/pallas_call | solution.py:373
  139.3 5.3 %shard_map.86 = (bf16[8,1024,256]{2,1,0:T(8,128)(2,1)}, f32[1024,256]{1,0:T(8,128)}, bf16[640,512]{1,0:T(8,128)(2,1)}) custom-call(bf16[8,1024,256]{2,1,0:T(8,128)(2,1)} %get-tuple-element.9.base, f32[1024,256]{1,0:T(8,128)} %get-tuple-element.10.moment, bf16[640,512]{1,0:T(8,128)(2,1)} %get-tuple-element.11.keys), custom_call_target="tpu_custom_call" | custom-call | bytes 12582912 | tf_op jit(solution)/shard_map/pallas_call | solution.py:419

commit v4 on v3

--- a/solution.py
+++ b/solution.py
@@ -148,14 +148,15 @@
         part = pl.ds(i * XR, XR)
         return pltpu.make_async_copy(acts.at[part], xbuf.at[part], load_x.at[i])
 
+    barrier = pltpu.get_barrier_semaphore()
+    for peer in (before, after, sibling, pair, *along):
+        pl.semaphore_signal(barrier, inc=1, device_id=peer, device_id_type=MESH)
+
     load_exps.start()
     for j in range(J):
         load_base(j).start()
         load_local(j).start()
 
-    barrier = pltpu.get_barrier_semaphore()
-    for peer in (before, after, sibling, pair, *along):
-        pl.semaphore_signal(barrier, inc=1, device_id=peer, device_id_type=MESH)
     pl.semaphore_wait(barrier, 6)
 
     gain_copy.start()

time: 146 us -> 146 us (level)
  no operation moved by 1% of the time
where the time goes in v4:
time: 146 us; the launch traced here: 145 us
  Pallas kernels  144 us (99%)
    pallas_call x1, Pallas kernels, shards(): pl.pallas_call(kernel, out_shape=(jax.ShapeDtypeStruct((REPLICAS, ROWS, K...  139 us
    pallas_call x1, Pallas kernels, shards(): pl.pallas_call(hand_on, out_shape=tuple((jax.ShapeDtypeStruct(out.shape,...  5.34 us

profile of v4, /device:TPU:24, one launch (start us, length us, event | category | flops | bytes accessed | tf_op | source)
XLA Modules:
  0.0 144.6 jit_solution(5812882905100537055)
XLA Ops:
  0.6 138.6 %shard_map.85 = (bf16[8,1024,256]{2,1,0:T(8,128)(2,1)}, f32[1024,256]{1,0:T(8,128)}, bf16[640,512]{1,0:T(8,128)(2,1)}) custom-call(bf16[8,1024,256]{2,1,0:T(8,128)(2,1)} %bitcast.9, bf16[8192,256]{1,0:T(8,128)(2,1)} %bitcast.10, f32[1024,256]{1,0:T(8,128)} %bitcast.11, s32[8,32,256]{2,1,0:T(8,128)} %bitcast.12, bf16[640,8192]{1,0:T(8,128)(2,1)} %bitcast.8, ...), custom_call_target="tpu_custom_call" | custom-call | flops 5368709120 | bytes 41943040 | tf_op jit(solution)/shard_map/pallas_call | solution.py:374
  139.3 5.3 %shard_map.86 = (bf16[8,1024,256]{2,1,0:T(8,128)(2,1)}, f32[1024,256]{1,0:T(8,128)}, bf16[640,512]{1,0:T(8,128)(2,1)}) custom-call(bf16[8,1024,256]{2,1,0:T(8,128)(2,1)} %get-tuple-element.9.base, f32[1024,256]{1,0:T(8,128)} %get-tuple-element.10.moment, bf16[640,512]{1,0:T(8,128)(2,1)} %get-tuple-element.11.keys), custom_call_target="tpu_custom_call" | custom-call | bytes 12582912 | tf_op jit(solution)/shard_map/pallas_call | solution.py:420
